TPU v7x, 32 devices: a whole 2x2x4 slice. The times are simulated.
32 devices in a mesh: dp: 16 (over z, y, core), tensor: 2 (over x).
Axes of the slice: x: 2, y: 2, z: 4, core: 2. Of those that a mesh axis runs over, the one named last changes fastest.
Arguments:
- block_in: bfloat16 [16384, 1024], P(('dp', 'tensor')), may hold values from -6 to 6
- segment_ids: int32 [16, 1024], P('dp'), may hold values from 0 to 3, never falling along the last dimension, each value on 1 to 512 neighbouring positions
- cotangent: bfloat16 [16384, 1024], P(('dp', 'tensor')), may hold values from -6 to 6
- attn_gain: bfloat16 [1024], P('tensor'), may hold values from 0.5 to 1.5
- attn_shift: bfloat16 [1024], P('tensor'), may hold values from -3 to 3
- mlp_gain: bfloat16 [1024], P('tensor'), may hold values from 0.5 to 1.5
- mlp_shift: bfloat16 [1024], P('tensor'), may hold values from -3 to 3
- qkv_weight: bfloat16 [3, 1024, 1024], P(None, 'dp', 'tensor'), may hold values from -0.1875 to 0.1875
- out_weight: bfloat16 [1024, 1024], P('tensor', 'dp'), may hold values from -1 to 1
- up_weight: bfloat16 [1024, 4096], P('dp', 'tensor'), may hold values from -0.1875 to 0.1875
- up_bias: bfloat16 [4096], P('tensor'), may hold values from -3 to 3
- down_weight: bfloat16 [4096, 1024], P('tensor', 'dp'), may hold values from -0.09375 to 0.09375
- out_bias: bfloat16 [1024], P('tensor'), may hold values from -3 to 3
Outputs:
- block_out: bfloat16 [16384, 1024], P(('dp', 'tensor'))
- grad_in: float32 [16384, 1024], P(('dp', 'tensor'))
- grad_attn_gain: float32 [1024], P('tensor')
- grad_attn_shift: float32 [1024], P('tensor')
- grad_mlp_gain: float32 [1024], P('tensor')
- grad_mlp_shift: float32 [1024], P('tensor')
- grad_qkv_weight: float32 [3, 1024, 1024], P(None, 'dp', 'tensor')
- grad_out_weight: float32 [1024, 1024], P('tensor', 'dp')
- grad_up_weight: float32 [1024, 4096], P('dp', 'tensor')
- grad_up_bias: float32 [4096], P('tensor')
- grad_down_weight: float32 [4096, 1024], P('tensor', 'dp')
- grad_out_bias: float32 [1024], P('tensor')
Inputs may be any that keep to these rules, and one draw needn't show every extreme that they name: `segment_ids`: document numbers never fall along a row; each document has at most half of 1024 tokens.
All inputs are finite; a program needn't handle non-finite values.
Results may differ from a plain program's by a relative error of at most 0.014.
Values may be sent and summed in bfloat16 or wider, within the bound.
A program may use at most 192 MiB of HBM per device.

v0:
```python
import math

import jax
import jax.numpy as jnp
from jax import lax
from jax.sharding import PartitionSpec as P

HD = 64
ROT = 16


EPS = 1e-05
MASKED = -1e30


def rope_tables(segment_rows):
    seq_count, length = segment_rows.shape
    col_index = lax.broadcasted_iota(jnp.int32, (seq_count, length), 1)
    starts_doc = jnp.concatenate(
        [jnp.ones((seq_count, 1), jnp.bool_), segment_rows[:, 1:] != segment_rows[:, :-1]], axis=1
    )
    doc_start = lax.cummax(jnp.where(starts_doc, col_index, 0), axis=1)
    doc_pos = (col_index - doc_start).reshape(seq_count * length).astype(jnp.float32)
    half_rot = ROT // 2
    freq_tab = 10000.0 ** (-(jnp.arange(half_rot, dtype=jnp.float32) * 2.0) / ROT)
    angles = doc_pos[:, None] * freq_tab[None, :]
    cos_tab = jnp.concatenate([jnp.cos(angles), jnp.cos(angles)], axis=1)
    sine_tab = jnp.concatenate([jnp.sin(angles), jnp.sin(angles)], axis=1)
    return (cos_tab[:, None, :], sine_tab[:, None, :])


def rotate_fwd(row_vals, cos_tab, sine_tab):
    half_rot = ROT // 2
    head_part = row_vals[..., :ROT]
    turned = jnp.concatenate([-head_part[..., half_rot:], head_part[..., :half_rot]], axis=-1)
    return jnp.concatenate([head_part * cos_tab + turned * sine_tab, row_vals[..., ROT:]], axis=-1)


def rotate_back(grad_vals, cos_tab, sine_tab):
    half_rot = ROT // 2
    head_part = grad_vals[..., :ROT]
    scaled = head_part * sine_tab
    turned = jnp.concatenate([scaled[..., half_rot:], -scaled[..., :half_rot]], axis=-1)
    return jnp.concatenate([head_part * cos_tab + turned, grad_vals[..., ROT:]], axis=-1)


def layer_stats(row_vals):
    mean_row = jnp.mean(row_vals, axis=-1, keepdims=True)
    centred = row_vals - mean_row
    inv_dev = lax.rsqrt(jnp.mean(centred * centred, axis=-1, keepdims=True) + EPS)
    return (centred * inv_dev, inv_dev)


def norm_back(grad_h, gain, normed, inv_dev):
    scaled = grad_h * gain
    return inv_dev * (
        scaled
        - jnp.mean(scaled, axis=-1, keepdims=True)
        - normed * jnp.mean(scaled * normed, axis=-1, keepdims=True)
    )


def gelu_exact(hidden_pre):
    return jax.nn.gelu(hidden_pre, approximate=False)


def masked_scores(queries, key_rows, seg_row):
    length = seg_row.shape[0]
    scores = jnp.einsum("qhd,khd->hqk", queries, key_rows, preferred_element_type=jnp.float32) * (
        1.0 / math.sqrt(HD)
    )
    row_pos = lax.broadcasted_iota(jnp.int32, (length, length), 0)
    col_pos = lax.broadcasted_iota(jnp.int32, (length, length), 1)
    allowed = (col_pos <= row_pos) & (seg_row[:, None] == seg_row[None, :])
    return jnp.where(allowed[None], scores, MASKED)


def attend_one(pieces):
    queries, key_rows, values, seg_row = pieces
    scores = masked_scores(queries, key_rows, seg_row)
    row_max = jnp.max(scores, axis=-1, keepdims=True)
    exp_terms = jnp.exp(scores - row_max)
    row_total = jnp.sum(exp_terms, axis=-1, keepdims=True)
    attn_probs = exp_terms / row_total
    mixture = jnp.einsum(
        "hqk,khd->qhd", attn_probs.astype(jnp.bfloat16), values, preferred_element_type=jnp.float32
    )
    return (mixture.astype(jnp.bfloat16), row_max + jnp.log(row_total))


def attend_back(pieces):
    queries, key_rows, values, seg_row, grad_mix, log_total = pieces
    scores = masked_scores(queries, key_rows, seg_row)
    attn_probs = jnp.exp(scores - log_total)
    grad_probs = jnp.einsum("qhd,khd->hqk", grad_mix, values, preferred_element_type=jnp.float32)
    grad_scores = (
        attn_probs * (grad_probs - jnp.sum(attn_probs * grad_probs, axis=-1, keepdims=True))
    ).astype(jnp.bfloat16)
    scale_qk = 1.0 / math.sqrt(HD)
    grad_values = jnp.einsum(
        "hqk,qhd->khd",
        attn_probs.astype(jnp.bfloat16),
        grad_mix,
        preferred_element_type=jnp.float32,
    )
    grad_queries = (
        jnp.einsum("hqk,khd->qhd", grad_scores, key_rows, preferred_element_type=jnp.float32)
        * scale_qk
    )
    grad_keys = (
        jnp.einsum("hqk,qhd->khd", grad_scores, queries, preferred_element_type=jnp.float32)
        * scale_qk
    )
    return (grad_queries, grad_keys, grad_values)


def per_device(
    block_in,
    segment_ids,
    cotangent,
    attn_gain,
    attn_shift,
    mlp_gain,
    mlp_shift,
    qkv_weight,
    out_weight,
    up_weight,
    up_bias,
    down_weight,
    out_bias,
):
    row_vals, cot_rows, gain_one, shift_one, gain_two, shift_two, bias_full = (
        lax.all_gather(block_in, "tensor", axis=0, tiled=True),
        lax.all_gather(cotangent, "tensor", axis=0, tiled=True),
        lax.all_gather(attn_gain, "tensor", axis=0, tiled=True),
        lax.all_gather(attn_shift, "tensor", axis=0, tiled=True),
        lax.all_gather(mlp_gain, "tensor", axis=0, tiled=True),
        lax.all_gather(mlp_shift, "tensor", axis=0, tiled=True),
        lax.all_gather(out_bias, "tensor", axis=0, tiled=True),
    )
    w_attn, w_proj, w_up, w_down = (
        lax.all_gather(qkv_weight, "dp", axis=1, tiled=True),
        lax.all_gather(out_weight, "dp", axis=1, tiled=True),
        lax.all_gather(up_weight, "dp", axis=0, tiled=True),
        lax.all_gather(down_weight, "dp", axis=1, tiled=True),
    )
    group_rows = row_vals.shape[0]
    own_rows = block_in.shape[0]
    seq_count, length = segment_ids.shape
    heads_here = w_attn.shape[2] // HD
    cos_tab, sine_tab = rope_tables(segment_ids)
    gain_one = gain_one.astype(jnp.float32)
    gain_two = gain_two.astype(jnp.float32)
    normed, inv_dev = layer_stats(row_vals.astype(jnp.float32))
    h_attn = (normed * gain_one + shift_one.astype(jnp.float32)).astype(jnp.bfloat16)
    h_mlp = (normed * gain_two + shift_two.astype(jnp.float32)).astype(jnp.bfloat16)
    projected = jnp.einsum("td,cde->cte", h_attn, w_attn, preferred_element_type=jnp.float32)
    shaped = projected.reshape(3, group_rows, heads_here, HD)
    queries = rotate_fwd(shaped[0], cos_tab, sine_tab).astype(jnp.bfloat16)
    key_rows = rotate_fwd(shaped[1], cos_tab, sine_tab).astype(jnp.bfloat16)
    values = shaped[2].astype(jnp.bfloat16)
    per_seq = (seq_count, length, heads_here, HD)
    seq_queries = queries.reshape(per_seq)
    seq_keys = key_rows.reshape(per_seq)
    seq_values = values.reshape(per_seq)
    mixture, log_total = lax.map(attend_one, (seq_queries, seq_keys, seq_values, segment_ids))
    attended = mixture.reshape(group_rows, heads_here * HD)
    hidden_pre = jnp.dot(h_mlp, w_up, preferred_element_type=jnp.float32) + up_bias.astype(
        jnp.float32
    )
    activated, gelu_pull = jax.vjp(gelu_exact, hidden_pre)
    act_low = activated.astype(jnp.bfloat16)
    partial_out = jnp.dot(attended, w_proj, preferred_element_type=jnp.float32) + jnp.dot(
        act_low, w_down, preferred_element_type=jnp.float32
    )
    summed = lax.psum_scatter(partial_out, "tensor", scatter_dimension=0, tiled=True)
    out_rows = (block_in.astype(jnp.float32) + bias_full.astype(jnp.float32) + summed).astype(
        jnp.bfloat16
    )
    w_attn, w_proj, w_up, w_down = (
        lax.all_gather(qkv_weight, "dp", axis=1, tiled=True),
        lax.all_gather(out_weight, "dp", axis=1, tiled=True),
        lax.all_gather(up_weight, "dp", axis=0, tiled=True),
        lax.all_gather(down_weight, "dp", axis=1, tiled=True),
    )
    grad_proj_w = jnp.einsum("te,td->ed", attended, cot_rows, preferred_element_type=jnp.float32)
    grad_down = jnp.einsum("tf,td->fd", act_low, cot_rows, preferred_element_type=jnp.float32)
    grad_act = jnp.einsum("td,fd->tf", cot_rows, w_down, preferred_element_type=jnp.float32)
    grad_pre = gelu_pull(grad_act)[0].astype(jnp.bfloat16)
    grad_bias_up = jnp.sum(grad_pre.astype(jnp.float32), axis=0)
    grad_up = jnp.einsum("td,tf->df", h_mlp, grad_pre, preferred_element_type=jnp.float32)
    grad_h_mlp = jnp.einsum("tf,df->td", grad_pre, w_up, preferred_element_type=jnp.float32)
    grad_mix = (
        jnp.einsum("td,ed->te", cot_rows, w_proj, preferred_element_type=jnp.float32)
        .astype(jnp.bfloat16)
        .reshape(per_seq)
    )
    grad_q, grad_k, grad_v = lax.map(
        attend_back, (seq_queries, seq_keys, seq_values, segment_ids, grad_mix, log_total)
    )
    flat_shape = (group_rows, heads_here, HD)
    grad_q = rotate_back(grad_q.reshape(flat_shape), cos_tab, sine_tab)
    grad_k = rotate_back(grad_k.reshape(flat_shape), cos_tab, sine_tab)
    grad_proj = (
        jnp.stack([grad_q, grad_k, grad_v.reshape(flat_shape)])
        .reshape(3, group_rows, heads_here * HD)
        .astype(jnp.bfloat16)
    )
    grad_attn_w = jnp.einsum("td,cte->cde", h_attn, grad_proj, preferred_element_type=jnp.float32)
    grad_h_attn = jnp.einsum("cte,cde->td", grad_proj, w_attn, preferred_element_type=jnp.float32)
    own_cot = cotangent.astype(jnp.float32)
    grad_bias_out = jnp.sum(own_cot, axis=0)
    grad_one, grad_two = (
        lax.psum_scatter(
            grad_h_attn.astype(jnp.bfloat16), "tensor", scatter_dimension=0, tiled=True
        ).astype(jnp.float32),
        lax.psum_scatter(
            grad_h_mlp.astype(jnp.bfloat16), "tensor", scatter_dimension=0, tiled=True
        ).astype(jnp.float32),
    )
    start_row = lax.axis_index("tensor") * own_rows
    own_normed = lax.dynamic_slice_in_dim(normed, start_row, own_rows, 0)
    own_inv = lax.dynamic_slice_in_dim(inv_dev, start_row, own_rows, 0)
    sum_gain_one, sum_shift_one, sum_gain_two, sum_shift_two, sum_bias_out = (
        lax.psum_scatter(
            jnp.sum(grad_one * own_normed, axis=0), "tensor", scatter_dimension=0, tiled=True
        ),
        lax.psum_scatter(jnp.sum(grad_one, axis=0), "tensor", scatter_dimension=0, tiled=True),
        lax.psum_scatter(
            jnp.sum(grad_two * own_normed, axis=0), "tensor", scatter_dimension=0, tiled=True
        ),
        lax.psum_scatter(jnp.sum(grad_two, axis=0), "tensor", scatter_dimension=0, tiled=True),
        lax.psum_scatter(grad_bias_out, "tensor", scatter_dimension=0, tiled=True),
    )
    grad_rows = (
        own_cot
        + norm_back(grad_one, gain_one, own_normed, own_inv)
        + norm_back(grad_two, gain_two, own_normed, own_inv)
    )
    sum_gain_one, sum_shift_one, sum_gain_two, sum_shift_two, sum_bias_out, sum_bias_up = lax.psum(
        (sum_gain_one, sum_shift_one, sum_gain_two, sum_shift_two, sum_bias_out, grad_bias_up), "dp"
    )
    shard_attn, shard_proj, shard_up, shard_down = (
        lax.psum_scatter(
            grad_attn_w.astype(jnp.bfloat16), "dp", scatter_dimension=1, tiled=True
        ).astype(jnp.float32),
        lax.psum_scatter(
            grad_proj_w.astype(jnp.bfloat16), "dp", scatter_dimension=1, tiled=True
        ).astype(jnp.float32),
        lax.psum_scatter(
            grad_up.astype(jnp.bfloat16), "dp", scatter_dimension=0, tiled=True
        ).astype(jnp.float32),
        lax.psum_scatter(
            grad_down.astype(jnp.bfloat16), "dp", scatter_dimension=1, tiled=True
        ).astype(jnp.float32),
    )
    return (
        out_rows,
        grad_rows,
        sum_gain_one,
        sum_shift_one,
        sum_gain_two,
        sum_shift_two,
        shard_attn,
        shard_proj,
        shard_up,
        sum_bias_up,
        shard_down,
        sum_bias_out,
    )


def solution(mesh):
    return jax.shard_map(
        per_device,
        mesh=mesh,
        in_specs=(
            P(("dp", "tensor"), None),
            P("dp", None),
            P(("dp", "tensor"), None),
            P("tensor"),
            P("tensor"),
            P("tensor"),
            P("tensor"),
            P(None, "dp", "tensor"),
            P("tensor", "dp"),
            P("dp", "tensor"),
            P("tensor"),
            P("tensor", "dp"),
            P("tensor"),
        ),
        out_specs=(
            P(("dp", "tensor"), None),
            P(("dp", "tensor"), None),
            P("tensor"),
            P("tensor"),
            P("tensor"),
            P("tensor"),
            P(None, "dp", "tensor"),
            P("tensor", "dp"),
            P("dp", "tensor"),
            P("tensor"),
            P("tensor", "dp"),
            P("tensor"),
        ),
        check_vma=False,
    )
```

profile of v0, /device:TPU:0, one launch (start us, length us, event | category | flops | bytes accessed | tf_op | source)
XLA Modules:
  0.0 779.6 jit_solution(9903986438125184240)
XLA Ops:
  27.0 18.4 %all-gather.12.cloned.1.call-done = bf16[1024,1024]{1,0:T(8,128)(2,1)} async-done(((bf16[512,1024]{1,0:T(8,128)(2,1)}), bf16[1024,1024]{1,0:T(8,128)(2,1)}) %all-gather.12.cloned.1.call-update) | async-done | bytes 2097168 | tf_op jit(solution)/shard_map/all_gather | solution.py:133
  49.8 35.8 %all-gather.16.cloned.1.call-done = bf16[512,1024]{0,1:T(8,128)(2,1)} async-done(((bf16[512,64]{0,1:T(8,128)(2,1)}), bf16[512,1024]{0,1:T(8,128)(2,1)}) %all-gather.16.cloned.1.call-update) | async-done | bytes 1048592 | tf_op jit(solution)/shard_map/all_gather | solution.py:143
  85.6 33.6 %all-gather.22.cloned.1.call-done = bf16[1024,1024]{1,0:T(8,128)(2,1)} async-done(((bf16[512,1024]{1,0:T(8,128)(2,1)}), bf16[1024,1024]{1,0:T(8,128)(2,1)}) %all-gather.22.cloned.1.call-update) | async-done | bytes 2097168 | tf_op jit(solution)/shard_map/all_gather | solution.py:134
  122.3 44.1 %all-gather.14.cloned.1.call-done = bf16[3,1024,512]{2,1,0:T(8,128)(2,1)} async-done(((bf16[3,64,512]{2,1,0:T(8,128)(2,1)}), bf16[3,1024,512]{2,1,0:T(8,128)(2,1)}) %all-gather.14.cloned.1.call-update) | async-done | bytes 3145744 | tf_op jit(solution)/shard_map/all_gather | solution.py:142
  174.7 13.8 %fusion.60 = (f32[8,1024]{1,0:T(8,128)S(1)}, f32[8,1024,1024]{1,2,0:T(8,128)}) fusion(bf16[1024,8,48]{0,2,1:T(8,128)(2,1)S(1)} %slice.153, bf16[1024,8,16]{0,2,1:T(8,128)(2,1)S(1)} %get-tuple-element.136, bf16[1024,8,48]{0,2,1:T(8,128)(2,1)S(1)} %slice.154, bf16[1024,8,16]{0,2,1:T(8,128)(2,1)S(1)} %get-tuple-element.135, pred[1024,1024]{0,1:T(8,128)(4,1)S(1)} %copy-done.14), kind=kOutput, calls=%fused_computation.134 | convolution fusion | flops 1103093760 | bytes 36732928 | tf_op jit(solution)/shard_map/while/body/eval_jaxpr/qhd,khd->hqk/dot_general | solution.py:69
  188.6 13.5 %fusion = f32[8,1024]{1,0:T(8,128)S(1)} fusion(f32[8,1024,1024]{1,2,0:T(8,128)} %get-tuple-element.144, f32[8,1024]{1,0:T(8,128)S(1)} %get-tuple-element.143), kind=kLoop, calls=%fused_computation.6 | loop fusion | flops 16769024 | bytes 33619968 | tf_op jit(solution)/shard_map/while/body/eval_jaxpr/reduce_sum | solution.py:83
  202.1 22.1 %multiply_reduce_fusion = (f32[8,1024]{1,0:T(8,128)S(1)}, f32[8,1024,1024]{1,2,0:T(8,128)}) fusion(f32[8,1024,1024]{1,2,0:T(8,128)} %get-tuple-element.144, f32[8,1024]{1,0:T(8,128)S(1)} %log_add_fusion, bf16[1024,8,64]{0,2,1:T(8,128)(2,1)S(1)} %bitcast.76, bf16[1024,8,64]{0,2,1:T(8,128)(2,1)S(1)} %bitcast.78), kind=kOutput, calls=%fused_computation.1 | convolution fusion | flops 1098899456 | bytes 69271552 | tf_op jit(solution)/shard_map/while/body/eval_jaxpr/qhd,khd->hqk/dot_general | solution.py:95
  224.2 29.0 %multiply_convert_fusion = bf16[8,1024,1024]{1,2,0:T(8,128)(2,1)} fusion(f32[8,1024,1024]{1,2,0:T(8,128)} %get-tuple-element.146, f32[8,1024,1024]{1,2,0:T(8,128)} %get-tuple-element.144, f32[8,1024]{1,0:T(8,128)S(1)} %get-tuple-element.145, f32[8,1024]{1,0:T(8,128)S(1)} %log_add_fusion), kind=kLoop, calls=%fused_computation | loop fusion | flops 33554432 | bytes 83951616 | tf_op jit(solution)/shard_map/while/body/eval_jaxpr/convert_element_type | solution.py:98
  253.2 9.2 %multiply_bitcast_fusion.1 = f32[1024,8,64]{0,2,1:T(8,128)S(1)} fusion(bf16[8,1024,1024]{1,2,0:T(8,128)(2,1)} %multiply_convert_fusion, bf16[1024,8,48]{0,2,1:T(8,128)(2,1)} %copy-done.7, bf16[1024,8,16]{0,2,1:T(8,128)(2,1)} %copy-done.10), kind=kOutput, calls=%fused_computation.71 | convolution fusion | flops 1076363264 | bytes 19922944 | tf_op jit(solution)/shard_map/while/body/eval_jaxpr/hqk,khd->qhd/dot_general | solution.py:107
  264.7 12.8 %multiply_bitcast_fusion = f32[1024,8,64]{0,2,1:T(8,128)} fusion(bf16[8,1024,1024]{1,2,0:T(8,128)(2,1)} %multiply_convert_fusion, bf16[1024,8,48]{0,2,1:T(8,128)(2,1)} %copy-done.8, bf16[1024,8,16]{0,2,1:T(8,128)(2,1)S(1)} %get-tuple-element.135), kind=kOutput, calls=%fused_computation.70 | convolution fusion | flops 1076363264 | bytes 19922944 | tf_op jit(solution)/shard_map/while/body/eval_jaxpr/hqk,qhd->khd/dot_general | solution.py:111
  290.7 14.3 %fusion.32 = bf16[8,64,1024]{2,1,0:T(8,128)(2,1)} fusion(bf16[1024,8,64]{0,2,1:T(8,128)(2,1)S(1)} %bitcast.77, f32[8,1024,1024]{1,2,0:T(8,128)} %get-tuple-element.144, f32[8,1024]{1,0:T(8,128)S(1)} %log_add_fusion), kind=kOutput, calls=%fused_computation.78 | convolution fusion | flops 1091043328 | bytes 35684352 | tf_op jit(solution)/shard_map/while/body/eval_jaxpr/hqk,qhd->khd/dot_general | solution.py:100
  322.7 14.4 %fusion.35 = bf16[8,64,1024]{2,1,0:T(8,128)(2,1)S(1)} fusion(bf16[1024,8,64]{0,2,1:T(8,128)(2,1)S(1)} %bitcast.79, f32[8,1024,1024]{1,2,0:T(8,128)} %get-tuple-element.144, f32[8,1024]{1,0:T(8,128)S(1)} %copy-done.22, f32[8,1024]{1,0:T(8,128)S(1)} %copy-done.20), kind=kOutput, calls=%fused_computation.81 | convolution fusion | flops 1099431936 | bytes 35717120 | tf_op jit(solution)/shard_map/while/body/eval_jaxpr/hqk,khd->qhd/dot_general | solution.py:85
  356.8 9.5 %fusion.36 = f32[1024,2048]{1,0:T(8,128)} fusion(bf16[1024,2048]{1,0:T(8,128)(2,1)} %all-gather.18.cloned.1.call-done, f32[1024]{0:T(1024)S(1)} %bitcast.98, f32[1024]{0:T(1024)S(1)} %bitcast.90, bf16[1024,1024]{1,0:T(8,128)(2,1)S(1)} %copy-done, f32[1024]{0:T(1024)S(1)} %add_rsqrt_fusion, f32[1024]{0:T(1024)S(1)} %broadcast_multiply_fusion), kind=kOutput, calls=%fused_computation.86 | convolution fusion | flops 4301258752 | bytes 14696448 | tf_op jit(solution)/shard_map/dot_general | solution.py:168
  366.3 27.7 %convert_reduce_fusion = (f32[2048]{0:T(1024)S(1)}, bf16[1024,2048]{1,0:T(8,128)(2,1)S(1)}, f32[1024,2048]{1,0:T(8,128)}) fusion(f32[1024,2048]{1,0:T(8,128)} %fusion.36, f32[2048]{0:T(1024)S(1)} %convert_element_type.134, bf16[1024,1024]{1,0:T(8,128)(2,1)} %all-gather.22.cloned.1.call-done, bf16[2048,1024]{0,1:T(8,128)(2,1)} %all-gather.20.cloned.1.call-done), kind=kOutput, calls=%fused_computation.13 | convolution fusion | flops 4452251648 | bytes 27279360 | tf_op jit(solution)/shard_map/td,fd->tf/dot_general | solution.py:188
  402.0 10.7 %multiply_convert_fusion.1 = bf16[1024,2048]{1,0:T(8,128)(2,1)} fusion(f32[1024,2048]{1,0:T(8,128)} %get-tuple-element.122, f32[1024,2048]{1,0:T(8,128)} %fusion.36, f32[2048]{0:T(1024)S(1)} %convert_element_type.134), kind=kLoop, calls=%fused_computation.15 | loop fusion | flops 8388608 | bytes 20979712 | tf_op jit(solution)/shard_map/convert_element_type | solution.py:172
  412.7 8.4 %convolution_convert_fusion = bf16[2048,1024]{0,1:T(8,128)(2,1)} fusion(bf16[1024,2048]{1,0:T(8,128)(2,1)} %multiply_convert_fusion.1, bf16[1024,1024]{1,0:T(8,128)(2,1)S(1)} %copy-done.31), kind=kOutput, calls=%fused_computation.39 | convolution fusion | flops 4297064448 | bytes 10485760 | tf_op jit(solution)/shard_map/tf,td->fd/dot_general | solution.py:187
  421.2 8.8 %convolution_convert_fusion.1 = bf16[1024,2048]{1,0:T(8,128)(2,1)} fusion(bf16[1024,2048]{1,0:T(8,128)(2,1)} %copy-done.34, f32[1024]{0:T(1024)S(1)} %bitcast.99, f32[1024]{0:T(1024)S(1)} %bitcast.91, bf16[1024,1024]{1,0:T(8,128)(2,1)S(1)} %copy-done, f32[1024]{0:T(1024)S(1)} %add_rsqrt_fusion, f32[1024]{0:T(1024)S(1)} %broadcast_multiply_fusion), kind=kOutput, calls=%fused_computation.40 | convolution fusion | flops 4303355904 | bytes 10502144 | tf_op jit(solution)/shard_map/td,tf->df/dot_general | solution.py:191
  430.0 7.7 fusion.61
  453.3 40.4 %reduce-scatter.13.cloned.1.call-done = bf16[512,64]{0,1:T(8,128)(2,1)} async-done(((bf16[512,1024]{0,1:T(8,128)(2,1)}), bf16[512,64]{0,1:T(8,128)(2,1)}) %reduce-scatter.13.cloned.1.call-update) | async-done | bytes 65552 | tf_op jit(solution)/shard_map/reduce_scatter | solution.py:247
  495.1 31.6 %reduce-scatter.9.cloned.1.call-done = bf16[512,1024]{1,0:T(8,128)(2,1)} async-done(((bf16[1024,1024]{1,0:T(8,128)(2,1)}), bf16[512,1024]{1,0:T(8,128)(2,1)}) %reduce-scatter.9.cloned.1.call-update) | async-done | bytes 1048592 | tf_op jit(solution)/shard_map/reduce_scatter | solution.py:214
  526.8 34.6 %reduce-scatter.11.cloned.1.call-done = bf16[512,1024]{1,0:T(8,128)(2,1)} async-done(((bf16[1024,1024]{1,0:T(8,128)(2,1)}), bf16[512,1024]{1,0:T(8,128)(2,1)}) %reduce-scatter.11.cloned.1.call-update) | async-done | bytes 1048592 | tf_op jit(solution)/shard_map/reduce_scatter | solution.py:217
  576.3 60.5 %all-reduce.6 = (f32[512]{0:T(512)}, f32[512]{0:T(512)}, f32[512]{0:T(512)}, f32[512]{0:T(512)}, f32[2048]{0:T(1024)}, /*index=5*/f32[512]{0:T(512)}) all-reduce(f32[512]{0:T(512)S(1)} %dynamic-slice.9, f32[512]{0:T(512)S(1)} %dynamic-slice.11, f32[512]{0:T(512)S(1)} %dynamic-slice.13, ...), channel_id=1, replica_groups=mesh['dp'=16,'tensor'=2] {'dp'}, use_global_device_ids=true, to_apply=%region_16.17 | all-reduce | flops 4608 | bytes 36864 | tf_op jit(solution)/shard_map/psum | solution.py:240
  640.4 73.8 %reduce-scatter.15.cloned.1.call-done = bf16[64,2048]{1,0:T(8,128)(2,1)} async-done(((bf16[1024,2048]{1,0:T(8,128)(2,1)}), bf16[64,2048]{1,0:T(8,128)(2,1)}) %reduce-scatter.15.cloned.1.call-update) | async-done | bytes 262160 | tf_op jit(solution)/shard_map/reduce_scatter | solution.py:250
  715.9 53.9 %reduce-scatter.7.cloned.1.call-done = f32[512,1024]{1,0:T(8,128)} async-done(((f32[1024,1024]{1,0:T(8,128)}), f32[512,1024]{1,0:T(8,128)}) %reduce-scatter.7.cloned.1.call-update) | async-done | bytes 2097168 | tf_op jit(solution)/shard_map/reduce_scatter | solution.py:176
  (181 shorter events, 134.9 us)
Async XLA Ops:
  7.2 38.2 %all-gather.12.cloned.1.call-start = ((), (), s32[]{:S(2)}) async-start(), calls=%async_computation.6 | async-start | bytes 3145728 | tf_op jit(solution)/shard_map/all_gather | solution.py:133
  7.9 77.7 %all-gather.16.cloned.1.call-start = ((), (), s32[]{:S(2)}) async-start(), calls=%async_computation.8 | async-start | bytes 1114112 | tf_op jit(solution)/shard_map/all_gather | solution.py:143
  8.7 110.5 %all-gather.22.cloned.1.call-start = ((), (), s32[]{:S(2)}) async-start(), calls=%async_computation.12 | async-start | bytes 3145728 | tf_op jit(solution)/shard_map/all_gather | solution.py:134
  9.4 157.1 %all-gather.14.cloned.1.call-start = ((), (), s32[]{:S(2)}) async-start(), calls=%async_computation.7 | async-start | bytes 3342336 | tf_op jit(solution)/shard_map/all_gather | solution.py:142
  10.0 346.8 %all-gather.18.cloned.1.call-start = ((), (), s32[]{:S(2)}) async-start(), calls=%async_computation.9 | async-start | bytes 4456448 | tf_op jit(solution)/shard_map/all_gather | solution.py:144
  10.6 355.8 %all-gather.20.cloned.1.call-start = ((), (), s32[]{:S(2)}) async-start(), calls=%async_computation.10 | async-start | bytes 4456448 | tf_op jit(solution)/shard_map/all_gather | solution.py:145
  11.1 440.2 %all-reduce.10.cloned.1.call-start = ((), (), s32[]{:S(2)}) async-start(), calls=%async_computation.18 | async-start | bytes 8388608
  17.1 289.8 %copy-start.23 = (f32[2,1,512]{2,1,0:T(1,128)}, f32[2,1,512]{2,1,0:T(1,128)S(1)}, u32[]{:S(2)}) copy-start(f32[2,1,512]{2,1,0:T(1,128)S(1)} %convert_element_type.157) | copy-start | bytes 12292
  47.3 119.1 %copy-start = (bf16[1024,1024]{1,0:T(8,128)(2,1)S(1)}, bf16[1024,1024]{1,0:T(8,128)(2,1)}, u32[]{:S(2)}) copy-start(bf16[1024,1024]{1,0:T(8,128)(2,1)} %all-gather.12.cloned.1.call-done) | copy-start | bytes 6291460
  172.9 15.6 %copy-start.8 = (bf16[1024,8,48]{0,2,1:T(8,128)(2,1)}, bf16[1024,8,48]{0,2,1:T(8,128)(2,1)S(1)}, u32[]{:S(2)}) copy-start(bf16[1024,8,48]{0,2,1:T(8,128)(2,1)S(1)} %slice.154) | copy-start | bytes 2359300
  173.1 29.0 %copy-start.3 = (bf16[1,1024,512]{1,2,0:T(8,128)(2,1)}, bf16[1,1024,512]{1,2,0:T(8,128)(2,1)S(1)}, u32[]{:S(2)}) copy-start(bf16[1,1024,512]{1,2,0:T(8,128)(2,1)S(1)} %slice.150) | copy-start | bytes 3145732
  173.6 15.0 %copy-start.10 = (bf16[1024,8,16]{0,2,1:T(8,128)(2,1)}, bf16[1024,8,16]{0,2,1:T(8,128)(2,1)S(1)}, u32[]{:S(2)}) copy-start(bf16[1024,8,16]{0,2,1:T(8,128)(2,1)S(1)} %get-tuple-element.136) | copy-start | bytes 786436
  202.1 22.1 %copy-start.21 = (f32[8,1024]{1,0:T(8,128)}, f32[8,1024]{1,0:T(8,128)S(1)}, u32[]{:S(2)}) copy-start(f32[8,1024]{1,0:T(8,128)S(1)} %fusion) | copy-start | bytes 98308
  322.6 171.0 %reduce-scatter.13.cloned.1.call-start = ((), (), s32[]{:S(2)}) async-start(), calls=%async_computation.15 | async-start | bytes 1114112 | tf_op jit(solution)/shard_map/reduce_scatter | solution.py:247
  322.7 15.4 %copy-start.30 = (bf16[1024,1024]{1,0:T(8,128)(2,1)S(1)}, bf16[1024,1024]{1,0:T(8,128)(2,1)}, u32[]{:S(2)}) copy-start(bf16[1024,1024]{1,0:T(8,128)(2,1)} %all-gather.22.cloned.1.call-done) | copy-start | bytes 6291460
  340.5 186.3 %reduce-scatter.9.cloned.1.call-start = ((), (), s32[]{:S(2)}) async-start(), calls=%async_computation.13 | async-start | bytes 3145728 | tf_op jit(solution)/shard_map/reduce_scatter | solution.py:214
  356.7 204.7 %reduce-scatter.11.cloned.1.call-start = ((), (), s32[]{:S(2)}) async-start(), calls=%async_computation.14 | async-start | bytes 3145728 | tf_op jit(solution)/shard_map/reduce_scatter | solution.py:217
  366.3 29.7 %copy-start.29 = (bf16[1024,2048]{1,0:T(8,128)(2,1)S(1)}, bf16[1024,2048]{1,0:T(8,128)(2,1)}, u32[]{:S(2)}) copy-start(bf16[1024,2048]{1,0:T(8,128)(2,1)} %all-gather.18.cloned.1.call-done) | copy-start | bytes 12582916
  401.7 236.9 %reduce-scatter.17.cloned.1.call-start = ((), (), s32[]{:S(2)}) async-start(), calls=%async_computation.17 | async-start | bytes 4456448 | tf_op jit(solution)/shard_map/reduce_scatter | solution.py:253
  421.1 293.0 %reduce-scatter.15.cloned.1.call-start = ((), (), s32[]{:S(2)}) async-start(), calls=%async_computation.16 | async-start | bytes 4456448 | tf_op jit(solution)/shard_map/reduce_scatter | solution.py:250
  430.0 339.9 %reduce-scatter.7.cloned.1.call-start = ((), (), s32[]{:S(2)}) async-start(), calls=%async_computation.11 | async-start | bytes 6291456 | tf_op jit(solution)/shard_map/reduce_scatter | solution.py:176
  441.1 120.2 %copy-start.24 = (f32[2,1,512]{2,1,0:T(1,128)S(1)}, f32[2,1,512]{2,1,0:T(1,128)}, u32[]{:S(2)}) copy-start(f32[2,1,512]{2,1,0:T(1,128)} %copy-done.23) | copy-start | bytes 12292
  451.3 113.9 %copy-start.6 = (bf16[512,1024]{1,0:T(8,128)(2,1)S(1)}, bf16[512,1024]{1,0:T(8,128)(2,1)}, u32[]{:S(2)}) copy-start(bf16[512,1024]{1,0:T(8,128)(2,1)} %param.15) | copy-start | bytes 3145732
  565.2 204.6 %copy-start.5 = (bf16[512,1024]{1,0:T(8,128)(2,1)S(1)}, bf16[512,1024]{1,0:T(8,128)(2,1)}, u32[]{:S(2)}) copy-start(bf16[512,1024]{1,0:T(8,128)(2,1)} %param.13) | copy-start | bytes 3145732
  (24 other events, 120.6 us)
Sparse Core Ops, SparseCore 0:
  9.6 35.7 all-gather.11
  47.6 37.9 all-gather.15
  87.1 32.0 all-gather.21
  121.2 45.2 all-gather.13
  168.5 49.3 all-gather.17
  219.9 49.0 all-gather.19
  322.7 110.4 all-reduce.9
  437.3 56.2 reduce-scatter.12
  495.9 30.8 reduce-scatter.8
  529.5 31.8 reduce-scatter.10
  565.2 73.3 reduce-scatter.16
  642.8 71.2 reduce-scatter.14
  716.4 53.3 reduce-scatter.6
where the time goes:
time: 787 us; the launch traced here: 780 us
  waiting for transfers between devices  372 us (47%)
  matrix products  183 us (23%)
  blocking collectives  90.4 us (11%)
  other arithmetic  87.4 us (11%)
  local copies, waits for them, and re-layouts  29.8 us (4%)
  between operations  16 us (2%)
    reduce_scatter x1, waiting for transfers between devices, per_device(): lax.psum_scatter(grad_up.astype(jnp.bfloat16), 'dp', scatter_dimension=0,...  73.8 us
    psum x1, blocking collectives, per_device(): lax.psum((sum_gain_one, sum_shift_one, sum_gain_two, sum_shift_two, sum_b...  60.5 us
    reduce_scatter x1, waiting for transfers between devices, per_device(): lax.psum_scatter(partial_out, 'tensor', scatter_dimension=0, tiled=True)  53.9 us
    all_gather x1, waiting for transfers between devices, per_device(): lax.all_gather(qkv_weight, 'dp', axis=1, tiled=True)  44.1 us
    reduce_scatter x1, waiting for transfers between devices, per_device(): lax.psum_scatter(grad_proj_w.astype(jnp.bfloat16), 'dp', scatter_dimensio...  40.4 us
    all_gather x1, waiting for transfers between devices, per_device(): lax.all_gather(out_weight, 'dp', axis=1, tiled=True)  35.8 us
    reduce_scatter x1, waiting for transfers between devices, per_device(): lax.psum_scatter(grad_h_mlp.astype(jnp.bfloat16), 'tensor', scatter_dimen...  34.6 us
    all_gather x1, waiting for transfers between devices, per_device(): lax.all_gather(cotangent, 'tensor', axis=0, tiled=True)  33.6 us
  transfers between devices with their start and end apart: 13, of which 10 were waited for; matrix products, arithmetic and copies ran while one was open for 37% of the time, Pallas kernels for 0%

commit v1 on v0

v1 whole, which is shorter than its diff:
```python
import functools
import math

import jax
import jax.numpy as jnp
from jax import lax
from jax.experimental import pallas as pl
from jax.experimental.pallas import tpu as pltpu
from jax.sharding import PartitionSpec as P

HD = 64
ROT = 16
PAIR = 128
Q_BLOCK = 256
SUBS = 2
EPS = 1e-05
MASKED = -1e30
MESH = pl.DeviceIdType.MESH
BF = jnp.bfloat16
F32 = jnp.float32


def nt_dot(a, b):
    return lax.dot_general(a, b, (((1,), (1,)), ((), ())), preferred_element_type=F32)


def nn_dot(a, b):
    return lax.dot_general(a, b, (((1,), (0,)), ((), ())), preferred_element_type=F32)


def tn_dot(a, b):
    return lax.dot_general(a, b, (((0,), (0,)), ((), ())), preferred_element_type=F32)


def spot_of(chip, n):
    odd, level = chip % 2, chip // 2
    return (1 - odd) * level + odd * (n - 1 - level)


def chip_of(spot, n):
    back = spot // (n // 2)
    return (1 - back) * (2 * spot) + back * (2 * (n - 1 - spot) + 1)


def places(n_dp, n_t):
    n = n_dp // 2
    dp, ten = lax.axis_index("dp"), lax.axis_index("tensor")
    core = dp % 2
    spot = spot_of(dp // 2, n)
    right = chip_of((spot + 1) % n, n) * 2 + core
    left = chip_of((spot + n - 1) % n, n) * 2 + core
    other = dp + 1 - 2 * core
    peers = [(ten + o) % n_t for o in range(1, n_t)]
    return n, dp, ten, core, spot, right, left, other, peers


def greet(ten, dp, right, left, other, peers):
    barrier = pltpu.get_barrier_semaphore()
    for to in (right, left, other):
        pl.semaphore_signal(barrier, inc=1, device_id=(to, ten), device_id_type=MESH)
    for peer in peers:
        pl.semaphore_signal(barrier, inc=1, device_id=(dp, peer), device_id_type=MESH)
    pl.semaphore_wait(barrier, 3 + len(peers))


def gather_kernel(
    n_dp, n_t, w_ref, x_ref, c_ref, p_ref, w_out, x_out, c_out, p_out,
    own_sem, t_send, t_recv, r_send, r_recv, p_send, p_recv,
):
    n, dp, ten, core, spot, right, left, other, peers = places(n_dp, n_t)
    rows, width = w_ref.shape
    piece = width // (2 * SUBS)
    greet(ten, dp, right, left, other, peers)

    def rows_at(chip):
        return pl.ds(pl.multiple_of((chip * 2 + core) * rows, rows), rows)

    pending = []
    mine = rows_at(dp // 2)
    for k, to in ((0, right), (1, left)):
        for sub in range(SUBS):
            chain = k * SUBS + sub
            cols = pl.ds(chain * piece, piece)
            copy = pltpu.make_async_remote_copy(
                src_ref=w_ref.at[:, cols], dst_ref=w_out.at[mine, cols],
                send_sem=r_send.at[chain, 0], recv_sem=r_recv.at[chain, 0],
                device_id=(to, ten), device_id_type=MESH,
            )
            copy.start()
            pending.append((copy, chain, 0))
    tcopies = []
    for o, peer in enumerate(peers):
        for a, (src, dst) in enumerate(((x_ref, x_out), (c_ref, c_out), (p_ref, p_out))):
            have = src.shape[0]
            copy = pltpu.make_async_remote_copy(
                src_ref=src,
                dst_ref=dst.at[pl.ds(pl.multiple_of(ten * have, have), have)],
                send_sem=t_send.at[o, a], recv_sem=t_recv.at[o, a],
                device_id=(dp, peer), device_id_type=MESH,
            )
            copy.start()
            tcopies.append(copy)
    pairs = []
    for chain in range(2 * SUBS):
        cols = pl.ds(chain * piece, piece)
        copy = pltpu.make_async_remote_copy(
            src_ref=w_ref.at[:, cols], dst_ref=w_out.at[mine, cols],
            send_sem=p_send.at[chain, 0], recv_sem=p_recv.at[chain, 0],
            device_id=(other, ten), device_id_type=MESH,
        )
        copy.start()
        pairs.append(copy)
    locals_ = [pltpu.make_async_copy(w_ref, w_out.at[mine], own_sem.at[0])]
    for a, (src, dst) in enumerate(((x_ref, x_out), (c_ref, c_out), (p_ref, p_out))):
        have = src.shape[0]
        locals_.append(
            pltpu.make_async_copy(
                src, dst.at[pl.ds(pl.multiple_of(ten * have, have), have)], own_sem.at[a + 1]
            )
        )
    for copy in locals_:
        copy.start()

    sends = list(copy for copy, _, _ in pending)
    held = {chain: copy for copy, chain, _ in pending}
    for step in range(1, n):
        for sub in range(SUBS):
            for k, to in ((0, right), (1, left)):
                chain = k * SUBS + sub
                cols = pl.ds(chain * piece, piece)
                held[chain].wait_recv()
                origin = (spot + n - step) % n if k == 0 else (spot + step) % n
                block = rows_at(chip_of(origin, n))
                if step < n - 1:
                    copy = pltpu.make_async_remote_copy(
                        src_ref=w_out.at[block, cols], dst_ref=w_out.at[block, cols],
                        send_sem=r_send.at[chain, step], recv_sem=r_recv.at[chain, step],
                        device_id=(to, ten), device_id_type=MESH,
                    )
                    copy.start()
                    held[chain] = copy
                    sends.append(copy)
                copy = pltpu.make_async_remote_copy(
                    src_ref=w_out.at[block, cols], dst_ref=w_out.at[block, cols],
                    send_sem=p_send.at[chain, step], recv_sem=p_recv.at[chain, step],
                    device_id=(other, ten), device_id_type=MESH,
                )
                copy.start()
                pairs.append(copy)
    for copy in sends:
        copy.wait_send()
    for copy in pairs:
        copy.wait()
    for copy in tcopies:
        copy.wait()
    for copy in locals_:
        copy.wait()


def gather_all(w_shard, x, cot, params, n_dp, n_t):
    n = n_dp // 2
    chains = 2 * SUBS
    any_spec = pl.BlockSpec(memory_space=pl.ANY)
    dma = pltpu.SemaphoreType.DMA
    return pl.pallas_call(
        functools.partial(gather_kernel, n_dp, n_t),
        out_shape=[
            jax.ShapeDtypeStruct((w_shard.shape[0] * n_dp, w_shard.shape[1]), BF),
            jax.ShapeDtypeStruct((x.shape[0] * n_t, x.shape[1]), BF),
            jax.ShapeDtypeStruct((x.shape[0] * n_t, x.shape[1]), BF),
            jax.ShapeDtypeStruct((params.shape[0] * n_t, params.shape[1]), BF),
        ],
        in_specs=[any_spec] * 4,
        out_specs=[any_spec] * 4,
        scratch_shapes=[
            dma((4,)), dma((n_t - 1, 3)), dma((n_t - 1, 3)),
            dma((chains, n - 1)), dma((chains, n - 1)), dma((chains, n)), dma((chains, n)),
        ],
        compiler_params=pltpu.CompilerParams(collective_id=0, has_side_effects=True),
        name="gather_all",
    )(w_shard, x, cot, params)


def scatter_kernel(
    n_dp, n_t, g_ref, o_ref, e_ref, g_out, o_out, e_out,
    mine, paired, landed, own_sem, t_send, t_recv, r_send, r_recv, p_send, p_recv,
):
    n, dp, ten, core, spot, right, left, other, peers = places(n_dp, n_t)
    rows, width = g_out.shape
    half = width // 2
    piece = half // SUBS
    greet(ten, dp, right, left, other, peers)

    def goal(k, step):
        return chip_of((spot + 2 * n - 1 - step) % n if k == 0 else (spot + 1 + step) % n, n)

    def rows_at(chip, whose):
        return pl.ds(pl.multiple_of((chip * 2 + whose) * rows, rows), rows)

    pairs, locals_ = {}, {}
    for step in range(n):
        for k in (0, 1):
            cols = pl.ds(k * half, half)
            pairs[k, step] = pltpu.make_async_remote_copy(
                src_ref=g_ref.at[rows_at(goal(k, step), 1 - core), cols],
                dst_ref=paired.at[k, step],
                send_sem=p_send.at[k, step], recv_sem=p_recv.at[k, step],
                device_id=(other, ten), device_id_type=MESH,
            )
            pairs[k, step].start()
            locals_[k, step] = pltpu.make_async_copy(
                g_ref.at[rows_at(goal(k, step), core), cols], mine.at[k, step],
                own_sem.at[k, step],
            )
            locals_[k, step].start()
    tcopies = []
    for o, peer in enumerate(peers):
        for a, (src, dst) in enumerate(((o_ref, o_out), (e_ref, e_out))):
            have = dst.shape[1]
            copy = pltpu.make_async_remote_copy(
                src_ref=src.at[pl.ds(pl.multiple_of(peer * have, have), have)],
                dst_ref=dst.at[o],
                send_sem=t_send.at[o, a], recv_sem=t_recv.at[o, a],
                device_id=(dp, peer), device_id_type=MESH,
            )
            copy.start()
            tcopies.append(copy)
    held, sends = {}, []
    for step in range(n):
        for sub in range(SUBS):
            cols = pl.ds(sub * piece, piece)
            for k, to in ((0, right), (1, left)):
                chain = k * SUBS + sub
                if sub == 0:
                    locals_[k, step].wait()
                    pairs[k, step].wait_recv()
                total = mine[k, step, :, cols].astype(F32) + paired[k, step, :, cols].astype(F32)
                if step > 0:
                    held[chain].wait_recv()
                    total = total + landed[chain, step - 1].astype(F32)
                if step == n - 1:
                    g_out[:, pl.ds(chain * piece, piece)] = total
                else:
                    mine[k, step, :, cols] = total.astype(BF)
                    copy = pltpu.make_async_remote_copy(
                        src_ref=mine.at[k, step, :, cols], dst_ref=landed.at[chain, step],
                        send_sem=r_send.at[chain, step], recv_sem=r_recv.at[chain, step],
                        device_id=(to, ten), device_id_type=MESH,
                    )
                    copy.start()
                    held[chain] = copy
                    sends.append(copy)
    for copy in sends:
        copy.wait_send()
    for copy in pairs.values():
        copy.wait_send()
    for copy in tcopies:
        copy.wait()


def scatter_all(grads, out_part, e_part, n_dp, n_t):
    n = n_dp // 2
    chains = 2 * SUBS
    rows, width = grads.shape[0] // n_dp, grads.shape[1]
    own = out_part.shape[0] // n_t
    any_spec = pl.BlockSpec(memory_space=pl.ANY)
    dma = pltpu.SemaphoreType.DMA
    parts = jax.ShapeDtypeStruct((n_t - 1, own, out_part.shape[1]), BF)
    return pl.pallas_call(
        functools.partial(scatter_kernel, n_dp, n_t),
        out_shape=[jax.ShapeDtypeStruct((rows, width), F32), parts, parts],
        in_specs=[any_spec] * 3,
        out_specs=[pl.BlockSpec(memory_space=pltpu.VMEM), any_spec, any_spec],
        scratch_shapes=[
            pltpu.VMEM((2, n, rows, width // 2), BF),
            pltpu.VMEM((2, n, rows, width // 2), BF),
            pltpu.VMEM((chains, n - 1, rows, width // chains), BF),
            dma((2, n)), dma((n_t - 1, 2)), dma((n_t - 1, 2)),
            dma((chains, n - 1)), dma((chains, n - 1)), dma((2, n)), dma((2, n)),
        ],
        compiler_params=pltpu.CompilerParams(
            collective_id=1, has_side_effects=True, vmem_limit_bytes=40 * 2**20
        ),
        name="scatter_all",
    )(grads, out_part, e_part)


def attend_kernel(
    q_ref, k_ref, v_ref, g_ref, cos_ref, lo_ref, hi_ref, segq_ref, segk_ref,
    att_ref, dproj_ref, dk_acc, dv_acc, dq_acc, q_s, k_s, v_s,
):
    j = pl.program_id(1)
    length = q_ref.shape[0]
    width = dproj_ref.shape[1] // 3
    back = ROT // 2
    cos, lo, hi = cos_ref[...], lo_ref[...], hi_ref[...]

    def turn(w, sign):
        up = pltpu.roll(w, PAIR - back, 1)
        down = pltpu.roll(w, back, 1)
        return w * cos + sign * (up * lo + down * hi)

    q_s[...] = (turn(q_ref[...], 1.0).astype(BF).astype(F32) * (1.0 / math.sqrt(HD))).astype(BF)
    k_s[...] = turn(k_ref[...], 1.0).astype(BF)
    v_s[...] = v_ref[...].astype(BF)
    dk_acc[...] = jnp.zeros_like(dk_acc)
    dv_acc[...] = jnp.zeros_like(dv_acc)
    first = lax.broadcasted_iota(jnp.int32, (Q_BLOCK, PAIR), 1) < HD
    reach = -(-(length // 2 - 1) // Q_BLOCK) * Q_BLOCK
    for start in range(0, length, Q_BLOCK):
        lo_key = max(0, start - reach)
        span = start + Q_BLOCK - lo_key
        keys = slice(lo_key, lo_key + span)
        rows = slice(start, start + Q_BLOCK)
        q_pos = start + lax.broadcasted_iota(jnp.int32, (Q_BLOCK, span), 0)
        k_pos = lo_key + lax.broadcasted_iota(jnp.int32, (Q_BLOCK, span), 1)
        allowed = (k_pos <= q_pos) & (segq_ref[rows, :] == segk_ref[0, :, keys])
        bias = jnp.where(allowed, 0.0, MASKED)
        q_blk, g_blk = q_s[rows, :], g_ref[rows, :]
        k_blk, v_blk = k_s[keys, :], v_s[keys, :]
        outs, dqs = [], []
        for head in (0, 1):
            pick = first if head == 0 else jnp.logical_not(first)
            q_one = jnp.where(pick, q_blk, jnp.zeros_like(q_blk))
            g_one = jnp.where(pick, g_blk, jnp.zeros_like(g_blk))
            scores = nt_dot(q_one, k_blk) + bias
            terms = jnp.exp(scores - jnp.max(scores, axis=-1, keepdims=True))
            probs = terms * (1.0 / jnp.sum(terms, axis=-1, keepdims=True))
            low = probs.astype(BF)
            outs.append(nn_dot(low, v_blk))
            weighed = nt_dot(g_one, v_blk)
            mean = jnp.sum(probs * weighed, axis=-1, keepdims=True)
            dscore = (probs * (weighed - mean)).astype(BF)
            dqs.append(nn_dot(dscore, k_blk))
            dk_acc[keys, :] += tn_dot(dscore, q_one)
            dv_acc[keys, :] += tn_dot(low, g_one)
        att_ref[rows, :] = jnp.where(first, outs[0], outs[1]).astype(BF)
        dq_acc[rows, :] = jnp.where(first, dqs[0], dqs[1])
    at = pl.multiple_of(j * PAIR, PAIR)
    dproj_ref[:, pl.ds(at, PAIR)] = turn(dq_acc[...] * (1.0 / math.sqrt(HD)), -1.0).astype(BF)
    dproj_ref[:, pl.ds(width + at, PAIR)] = turn(dk_acc[...], -1.0).astype(BF)
    dproj_ref[:, pl.ds(2 * width + at, PAIR)] = dv_acc[...].astype(BF)


def attend(projected, grad_mix, tables, segment_ids):
    seqs, length = segment_ids.shape
    tokens, width = grad_mix.shape
    pairs = width // PAIR
    seg_col = segment_ids.reshape(tokens, 1)
    seg_row = segment_ids.reshape(seqs, 1, length)

    def col(at):
        return pl.BlockSpec((length, PAIR), lambda s, j: (s, j + at * pairs))

    table = pl.BlockSpec((length, PAIR), lambda s, j: (s, 0))
    return pl.pallas_call(
        attend_kernel,
        grid=(seqs, pairs),
        out_shape=[
            jax.ShapeDtypeStruct((tokens, width), BF),
            jax.ShapeDtypeStruct((tokens, 3 * width), BF),
        ],
        in_specs=[
            col(0), col(1), col(2), col(0), table, table, table,
            pl.BlockSpec((length, 1), lambda s, j: (s, 0)),
            pl.BlockSpec((1, 1, length), lambda s, j: (s, 0, 0)),
        ],
        out_specs=[col(0), pl.BlockSpec((length, 3 * width), lambda s, j: (s, 0))],
        scratch_shapes=[pltpu.VMEM((length, PAIR), F32)] * 3
        + [pltpu.VMEM((length, PAIR), BF)] * 3,
        compiler_params=pltpu.CompilerParams(vmem_limit_bytes=48 * 2**20),
        name="attend",
    )(projected, projected, projected, grad_mix, *tables, seg_col, seg_row)


def hidden_kernel(h_ref, c_ref, up_ref, down_ref, b_ref, act_ref, pre_ref, sum_ref):
    hidden = nn_dot(h_ref[...], up_ref[...]) + b_ref[...]
    pulled = nn_dot(c_ref[...], down_ref[...])
    phi = 0.5 + 0.5 * lax.erf(hidden * math.sqrt(0.5))
    act_ref[...] = (hidden * phi).astype(BF)
    density = jnp.exp(-0.5 * hidden * hidden) * (1.0 / math.sqrt(2.0 * math.pi))
    pre = (pulled * (phi + hidden * density)).astype(BF)
    pre_ref[...] = pre
    sum_ref[...] = jnp.sum(pre.astype(F32), axis=0, keepdims=True)


def hidden_branch(h_mlp, cot, weights, up_at, down_at, up_bias):
    tokens, model = h_mlp.shape
    ff = up_bias.shape[1]
    tile, chunk = 256, 1024
    return pl.pallas_call(
        hidden_kernel,
        grid=(tokens // chunk, ff // tile),
        out_shape=[
            jax.ShapeDtypeStruct((tokens, ff), BF),
            jax.ShapeDtypeStruct((tokens, ff), BF),
            jax.ShapeDtypeStruct((tokens // chunk, 1, ff), F32),
        ],
        in_specs=[
            pl.BlockSpec((chunk, model), lambda s, j: (s, 0)),
            pl.BlockSpec((chunk, model), lambda s, j: (s, 0)),
            pl.BlockSpec((model, tile), lambda s, j: (0, up_at // tile + j)),
            pl.BlockSpec((model, tile), lambda s, j: (0, down_at // tile + j)),
            pl.BlockSpec((1, tile), lambda s, j: (0, j)),
        ],
        out_specs=[
            pl.BlockSpec((chunk, tile), lambda s, j: (s, j)),
            pl.BlockSpec((chunk, tile), lambda s, j: (s, j)),
            pl.BlockSpec((None, 1, tile), lambda s, j: (s, 0, j)),
        ],
        compiler_params=pltpu.CompilerParams(vmem_limit_bytes=48 * 2**20),
        name="hidden_branch",
    )(h_mlp, cot, weights, weights, up_bias)


def rope_tables(segment_rows):
    seqs, length = segment_rows.shape
    col_index = lax.broadcasted_iota(jnp.int32, (seqs, length), 1)
    starts_doc = jnp.concatenate(
        [jnp.ones((seqs, 1), jnp.bool_), segment_rows[:, 1:] != segment_rows[:, :-1]], axis=1
    )
    doc_start = lax.cummax(jnp.where(starts_doc, col_index, 0), axis=1)
    doc_pos = (col_index - doc_start).reshape(seqs * length).astype(F32)
    half = ROT // 2
    freq = 10000.0 ** (-(jnp.arange(half, dtype=F32) * 2.0) / ROT)
    angles = doc_pos[:, None] * freq[None, :]
    cos, sine = jnp.cos(angles), jnp.sin(angles)
    zero = jnp.zeros_like(cos)
    one_rest = jnp.ones((seqs * length, HD - ROT), F32)
    zero_rest = jnp.zeros((seqs * length, HD - ROT), F32)
    reps = (1, PAIR // HD)
    return (
        jnp.tile(jnp.concatenate([cos, cos, one_rest], axis=1), reps),
        jnp.tile(jnp.concatenate([-sine, zero, zero_rest], axis=1), reps),
        jnp.tile(jnp.concatenate([zero, sine, zero_rest], axis=1), reps),
    )


def per_device(
    n_dp, n_t, block_in, segment_ids, cotangent, attn_gain, attn_shift, mlp_gain, mlp_shift,
    qkv_weight, out_weight, up_weight, up_bias, down_weight, out_bias,
):
    ten = lax.axis_index("tensor")
    wide, ff = out_weight.shape[0], up_weight.shape[1]
    own_rows, model = block_in.shape
    share = model // n_t
    w_shard = jnp.concatenate(
        [qkv_weight[0], qkv_weight[1], qkv_weight[2], out_weight.T, up_weight, down_weight.T],
        axis=1,
    )
    vectors = jnp.stack([attn_gain, attn_shift, mlp_gain, mlp_shift, out_bias])
    vectors = jnp.pad(vectors, ((0, 11), (0, 0)))
    w_all, rows_in, cot_rows, vec_all = gather_all(
        w_shard, block_in, cotangent, vectors, n_dp, n_t
    )
    vec_all = vec_all.reshape(n_t, 16, share).transpose(1, 0, 2).reshape(16, model).astype(F32)
    gain_one, shift_one, gain_two, shift_two, bias_out = (vec_all[i] for i in range(5))
    at_out, at_up, at_down = 3 * wide, 4 * wide, 4 * wide + ff
    w_qkv, w_out = w_all[:, :at_out], w_all[:, at_out:at_up]
    w_up, w_down = w_all[:, at_up:at_down], w_all[:, at_down:]
    tables = rope_tables(segment_ids)

    vals = rows_in.astype(F32)
    mean_row = jnp.mean(vals, axis=-1, keepdims=True)
    centred = vals - mean_row
    inv_dev = lax.rsqrt(jnp.mean(centred * centred, axis=-1, keepdims=True) + EPS)
    normed = centred * inv_dev
    h_attn = (normed * gain_one + shift_one).astype(BF)
    h_mlp = (normed * gain_two + shift_two).astype(BF)

    projected = nn_dot(h_attn, w_qkv)
    grad_mix = nn_dot(cot_rows, w_out).astype(BF)
    attended, grad_proj = attend(projected, grad_mix, tables, segment_ids)
    act, grad_pre, up_sums = hidden_branch(
        h_mlp, cot_rows, w_all, at_up, at_down, up_bias.astype(F32).reshape(1, ff)
    )
    partial_out = (nt_dot(attended, w_out) + nt_dot(act, w_down)).astype(BF)

    grad_one = nt_dot(grad_proj, w_qkv)
    grad_two = nt_dot(grad_pre, w_up)
    e_part = (grad_one * gain_one + grad_two * gain_two).astype(BF)
    own_cot = cotangent.astype(F32)
    placed = lax.dynamic_update_slice(
        jnp.zeros((n_t * ff,), F32), jnp.sum(up_sums, axis=(0, 1)), (ten * ff,)
    )
    small = jnp.concatenate([
        jnp.sum(grad_one * normed, axis=0), jnp.sum(grad_one, axis=0),
        jnp.sum(grad_two * normed, axis=0), jnp.sum(grad_two, axis=0),
        jnp.sum(own_cot, axis=0), placed,
    ])
    small = lax.psum(small, ("dp", "tensor"))

    grads = jnp.concatenate(
        [
            tn_dot(h_attn, grad_proj).astype(BF), tn_dot(cot_rows, attended).astype(BF),
            tn_dot(h_mlp, grad_pre).astype(BF), tn_dot(cot_rows, act).astype(BF),
        ],
        axis=1,
    )
    shard, out_got, e_got = scatter_all(grads, partial_out, e_part, n_dp, n_t)

    start = ten * own_rows
    def own(array):
        return lax.dynamic_slice_in_dim(array, start, own_rows, 0)

    summed = own(partial_out).astype(F32) + jnp.sum(out_got.astype(F32), axis=0)
    out_rows = (block_in.astype(F32) + bias_out + summed).astype(BF)
    e_sum = own(e_part).astype(F32) + jnp.sum(e_got.astype(F32), axis=0)
    own_normed, own_inv = own(normed), own(inv_dev)
    grad_rows = own_cot + own_inv * (
        e_sum
        - jnp.mean(e_sum, axis=-1, keepdims=True)
        - own_normed * jnp.mean(e_sum * own_normed, axis=-1, keepdims=True)
    )

    def part(index):
        return lax.dynamic_slice_in_dim(small, index * model + ten * share, share, 0)

    up_grad_bias = lax.dynamic_slice_in_dim(small, 5 * model + ten * ff, ff, 0)
    shard_qkv = jnp.stack([shard[:, c * wide : (c + 1) * wide] for c in range(3)])
    return (
        out_rows, grad_rows, part(0), part(1), part(2), part(3),
        shard_qkv, shard[:, at_out:at_up].T, shard[:, at_up:at_down],
        up_grad_bias, shard[:, at_down:].T, part(4),
    )


def solution(mesh):
    n_dp, n_t = mesh.shape["dp"], mesh.shape["tensor"]
    both = P(("dp", "tensor"), None)
    vec = P("tensor")
    return jax.shard_map(
        functools.partial(per_device, n_dp, n_t),
        mesh=mesh,
        in_specs=(
            both, P("dp", None), both, vec, vec, vec, vec,
            P(None, "dp", "tensor"), P("tensor", "dp"), P("dp", "tensor"), vec,
            P("tensor", "dp"), vec,
        ),
        out_specs=(
            both, both, vec, vec, vec, vec,
            P(None, "dp", "tensor"), P("tensor", "dp"), P("dp", "tensor"), vec,
            P("tensor", "dp"), vec,
        ),
        check_vma=False,
    )
```

time: 787 us -> 350 us (0.44)
  waiting for transfers between devices: 372 us -> 0 us
  Pallas kernels: 0 us -> 213 us
  matrix products: 183 us -> 55.1 us
  other arithmetic: 87.4 us -> 23.1 us
  blocking collectives: 90.4 us -> 40 us
  local copies, waits for them, and re-layouts: 29.8 us -> 13 us
  between operations: 16 us -> 1.53 us
    reduce_scatter x6 -> x0, waiting for transfers between devices: 236 us -> none  [the longest x1 73.8 us: per_device(): lax.psum_scatter(grad_up.astype(jnp.bfloat16), 'dp', scatter_dimension=0,...]
    pallas_call x0 -> x4, Pallas kernels: none -> 213 us  [the longest x1 93.1 us: gather_all(): pl.pallas_call(functools.partial(gather_kernel, n_dp, n_t), out_shape=[ja...]
    all_gather x6 -> x0, waiting for transfers between devices: 132 us -> none  [the longest x1 44.1 us: per_device(): lax.all_gather(qkv_weight, 'dp', axis=1, tiled=True)]
    dot_general x18 -> x10, matrix products: 183 us -> 55.1 us  [the longest x4 26.6 us: nt_dot(): lax.dot_general(a, b, (((1,), (1,)), ((), ())), preferred_element_type=F32)]
    convert_element_type x14 -> x4, other arithmetic: 48.8 us -> 2.47 us  [the longest x1 1.64 us: per_device(): out_rows = (block_in.astype(F32) + bias_out + summed).astype(BF)]
    all_gather x5 -> x0, blocking collectives: 22.8 us -> none  [the longest x1 5.22 us: per_device(): lax.all_gather(attn_gain, 'tensor', axis=0, tiled=True)]
    psum x1, blocking collectives: 60.5 us -> 40 us  [per_device(): small = lax.psum(small, ('dp', 'tensor'))]
    reduce_sum x5 -> x4, other arithmetic: 25.2 us -> 6.97 us  [the longest x1 2.28 us: per_device(): jnp.mean(centred * centred, axis=-1, keepdims=True) + EPS]
  transfers between devices with their start and end apart: 13 -> 0, of which waited for: 10 -> 0; matrix products, arithmetic and copies ran while one was open for 37% -> 0% of each run, Pallas kernels for 0% -> 0%
where the time goes in v1:
time: 350 us; the launch traced here: 345 us
  Pallas kernels  213 us (61%)
  matrix products  55.1 us (16%)
  blocking collectives  40 us (11%)
  other arithmetic  23.1 us (7%)
  local copies, waits for them, and re-layouts  13 us (4%)
    pallas_call x1, Pallas kernels, gather_all(): pl.pallas_call(functools.partial(gather_kernel, n_dp, n_t), out_shape=[ja...  93.1 us
    pallas_call x1, Pallas kernels, scatter_all(): pl.pallas_call(functools.partial(scatter_kernel, n_dp, n_t), out_shape=[j...  65.6 us
    psum x1, blocking collectives, per_device(): small = lax.psum(small, ('dp', 'tensor'))  40 us
    pallas_call x1, Pallas kernels, attend(): pl.pallas_call(attend_kernel, grid=(seqs, pairs), out_shape=[jax.ShapeDty...  38.3 us
    dot_general x4, matrix products, nt_dot(): lax.dot_general(a, b, (((1,), (1,)), ((), ())), preferred_element_type=F32)  26.6 us
    dot_general x4, matrix products, tn_dot(): lax.dot_general(a, b, (((0,), (0,)), ((), ())), preferred_element_type=F32)  18.2 us
    pallas_call x1, Pallas kernels, hidden_branch(): pl.pallas_call(hidden_kernel, grid=(tokens // chunk, ff // tile), out_sha...  15.5 us
    concatenate x1, other arithmetic, per_device(): jnp.concatenate([tn_dot(h_attn, grad_proj).astype(BF), tn_dot(cot_rows, a...  10.4 us

profile of v1, /device:TPU:0, one launch (start us, length us, event | category | flops | bytes accessed | tf_op | source)
XLA Modules:
  0.0 345.3 jit_solution(17062646948727954625)
XLA Ops:
  7.5 0.9 copy.29.segq_ref
  9.3 0.9 bitcast_dynamic-update-slice_fusion.4
  12.0 0.9 copy-done.6
  12.8 93.1 %gather_all.1 = (bf16[1024,6144]{1,0:T(8,128)(2,1)}, bf16[1024,1024]{1,0:T(8,128)(2,1)}, bf16[1024,1024]{1,0:T(8,128)(2,1)}, bf16[32,512]{1,0:T(8,128)(2,1)}) custom-call(bf16[64,6144]{1,0:T(8,128)(2,1)} %copy-done.6, bf16[512,1024]{1,0:T(8,128)(2,1)} %x_ref.1, bf16[512,1024]{1,0:T(8,128)(2,1)} %c_ref.1, bf16[16,512]{1,0:T(8,128)(2,1)} %pad.4.p_ref), custom_call_target="tpu_custom_call" | custom-call | tf_op jit(solution)/shard_map/gather_all/pallas_call | solution.py:165
  106.0 2.1 convert_reduce_fusion
  108.1 2.3 fusion.2
  110.5 2.6 convolution_convert_fusion.4.g_ref
  114.0 7.7 %fusion.9.q_ref.k_ref.v_ref = f32[1024,1536]{1,0:T(8,128)} fusion(bf16[1024,6144]{1,0:T(8,128)(2,1)} %get-tuple-element.26.up_ref.down_ref, bf16[1024,1024]{1,0:T(8,128)(2,1)S(1)} %copy-done.2, f32[1024]{0:T(1024)S(1)} %bitcast.84, f32[1024]{0:T(1024)S(1)} %bitcast.81, f32[1024]{0:T(1024)S(1)} %add_rsqrt_fusion, f32[1024]{0:T(1024)S(1)} %broadcast_multiply_fusion), kind=kOutput, calls=%fused_computation.21 | convolution fusion | flops 3227516928 | bytes 11550720 | tf_op jit(solution)/shard_map/dot_general | solution.py:28
  121.7 38.3 %attend.1 = (bf16[1024,512]{1,0:T(8,128)(2,1)S(1)}, bf16[1024,1536]{1,0:T(8,128)(2,1)}) custom-call(f32[1024,1536]{1,0:T(8,128)} %fusion.9.q_ref.k_ref.v_ref, f32[1024,1536]{1,0:T(8,128)} %fusion.9.q_ref.k_ref.v_ref, f32[1024,1536]{1,0:T(8,128)} %fusion.9.q_ref.k_ref.v_ref, bf16[1024,512]{1,0:T(8,128)(2,1)S(1)} %convolution_convert_fusion.4.g_ref, ...), custom_call_target="tpu_custom_call" | custom-call | tf_op jit(solution)/shard_map/attend/pallas_call | solution.py:356
  160.0 2.2 convolution_convert_fusion.3
  162.2 4.0 %convolution_convert_fusion = bf16[1024,1536]{1,0:T(8,128)(2,1)S(1)} fusion(bf16[1024,1536]{1,0:T(8,128)(2,1)S(1)} %copy-done.12, bf16[1024,1024]{1,0:T(8,128)(2,1)S(1)} %copy-done.2, f32[1024]{0:T(1024)S(1)} %bitcast.85, f32[1024]{0:T(1024)S(1)} %bitcast.82, f32[1024]{0:T(1024)S(1)} %add_rsqrt_fusion, f32[1024]{0:T(1024)S(1)} %broadcast_multiply_fusion), kind=kOutput, calls=%fused_computation.16 | convolution fusion | flops 3229089792 | bytes 8404992 | tf_op jit(solution)/shard_map/dot_general | solution.py:32
  166.2 7.1 %fusion.7 = f32[1024,1024]{1,0:T(8,128)} fusion(bf16[1024,1536]{1,0:T(8,128)(2,1)S(1)} %copy-done.12, bf16[1024,6144]{1,0:T(8,128)(2,1)} %get-tuple-element.26.up_ref.down_ref), kind=kOutput, calls=%fused_computation.19 | convolution fusion | flops 3221225472 | bytes 10485760 | tf_op jit(solution)/shard_map/dot_general | solution.py:24
  173.3 15.5 %hidden_branch.1 = (bf16[1024,2048]{1,0:T(8,128)(2,1)}, bf16[1024,2048]{1,0:T(8,128)(2,1)}, f32[1,1,2048]{2,1,0:T(1,128)S(1)}) custom-call(bf16[1024,1024]{1,0:T(8,128)(2,1)S(1)} %add_convert_fusion.2.h_ref, bf16[1024,1024]{1,0:T(8,128)(2,1)S(1)} %copy-done, bf16[1024,6144]{1,0:T(8,128)(2,1)} %get-tuple-element.26.up_ref.down_ref, ...), custom_call_target="tpu_custom_call" | custom-call | tf_op jit(solution)/shard_map/hidden_branch/pallas_call | solution.py:391
  189.1 10.2 %fusion.19 = (f32[1024]{0:T(1024)S(1)}, f32[1024]{0:T(1024)S(1)}, bf16[1024,1024]{1,0:T(8,128)(2,1)S(1)}, f32[1024]{0:T(1024)S(1)}, f32[1024]{0:T(1024)S(1)}, /*index=5*/f32[1024,1024]{1,0:T(8,128)S(1)}) fusion(f32[1024]{0:T(1024)S(1)} %add_rsqrt_fusion, f32[1024]{0:T(1024)S(1)} %broadcast_multiply_fusion, bf16[1024,1024]{1,0:T(8,128)(2,1)S(1)} %copy-done.2, ...), kind=kOutput, calls=%fused_computation.73 | convolution fusion | flops 4308594688 | bytes 21004288 | tf_op jit(solution)/shard_map/dot_general | solution.py:24
  199.3 7.2 %convolution_convert_fusion.2 = bf16[1024,2048]{1,0:T(8,128)(2,1)S(1)} fusion(bf16[1024,1024]{1,0:T(8,128)(2,1)S(1)} %add_convert_fusion.2.h_ref, bf16[1024,2048]{1,0:T(8,128)(2,1)} %get-tuple-element.31), kind=kOutput, calls=%fused_computation.18 | convolution fusion | flops 4297064448 | bytes 10485760 | tf_op jit(solution)/shard_map/dot_general | solution.py:32
  206.6 4.9 %convolution_convert_fusion.1 = bf16[1024,2048]{1,0:T(8,128)(2,1)S(1)} fusion(bf16[1024,1024]{1,0:T(8,128)(2,1)S(1)} %copy-done, bf16[1024,2048]{1,0:T(8,128)(2,1)S(1)} %copy-done.11), kind=kOutput, calls=%fused_computation.17 | convolution fusion | flops 4297064448 | bytes 10485760 | tf_op jit(solution)/shard_map/dot_general | solution.py:32
  211.4 6.7 %fusion.5 = f32[1024,1024]{1,0:T(8,128)S(1)} fusion(bf16[1024,2048]{1,0:T(8,128)(2,1)S(1)} %copy-done.11, bf16[1024,6144]{1,0:T(8,128)(2,1)} %get-tuple-element.26.up_ref.down_ref), kind=kOutput, calls=%fused_computation.12 | convolution fusion | flops 4294967296 | bytes 12582912 | tf_op jit(solution)/shard_map/dot_general | solution.py:24
  218.1 2.6 add_convert_fusion.1.o_ref
  220.7 10.4 %pad_maximum_fusion.g_ref = bf16[1024,6144]{1,0:T(8,128)(2,1)} fusion(bf16[1024,2048]{1,0:T(8,128)(2,1)S(1)} %convolution_convert_fusion.1, bf16[1024,2048]{1,0:T(8,128)(2,1)S(1)} %convolution_convert_fusion.2, bf16[1024,512]{1,0:T(8,128)(2,1)S(1)} %copy-done.5, bf16[1024,1536]{1,0:T(8,128)(2,1)S(1)} %convolution_convert_fusion), kind=kLoop, calls=%fused_computation | loop fusion | flops 50331648 | bytes 25165824 | tf_op jit(solution)/shard_map/concatenate | solution.py:493
  231.1 65.6 %scatter_all.1 = (f32[64,6144]{1,0:T(8,128)S(1)}, bf16[1,512,1024]{2,1,0:T(8,128)(2,1)S(1)}, bf16[1,512,1024]{2,1,0:T(8,128)(2,1)S(1)}) custom-call(bf16[1024,6144]{1,0:T(8,128)(2,1)} %pad_maximum_fusion.g_ref, bf16[1024,1024]{1,0:T(8,128)(2,1)S(1)} %add_convert_fusion.1.o_ref, bf16[1024,1024]{1,0:T(8,128)(2,1)S(1)} %get-tuple-element.42.e_ref), custom_call_target="tpu_custom_call" | custom-call | tf_op jit(solution)/shard_map/scatter_all/pallas_call | solution.py:269
  296.8 1.6 fusion.12
  299.0 2.1 convert_reduce_fusion.1
  301.1 40.0 %psum.7 = f32[9216]{0:T(1024)S(1)} all-reduce(f32[9216]{0:T(1024)S(1)} %constant_dynamic-update-slice_fusion.5), channel_id=1, replica_groups=mesh['dp'=16,'tensor'=2] {'dp','tensor'}, use_global_device_ids=true, to_apply=%region_11.12 | all-reduce | flops 9216 | bytes 73728 | tf_op jit(solution)/shard_map/psum | solution.py:491
  343.1 1.0 slice_bitcast_fusion
  (82 shorter events, 13.9 us)
Async XLA Ops:
  0.6 11.3 %copy-start.8 = (bf16[2048,64]{0,1:T(8,128)(2,1)S(1)}, bf16[2048,64]{0,1:T(8,128)(2,1)}, u32[]{:S(2)}) copy-start(bf16[2048,64]{0,1:T(8,128)(2,1)} %param.24) | copy-start | bytes 786436
  0.7 11.2 %copy-start.7 = (bf16[64,2048]{1,0:T(8,128)(2,1)S(1)}, bf16[64,2048]{1,0:T(8,128)(2,1)}, u32[]{:S(2)}) copy-start(bf16[64,2048]{1,0:T(8,128)(2,1)} %param.22) | copy-start | bytes 786436
  0.7 11.2 %copy-start.9 = (bf16[512,64]{0,1:T(8,128)(2,1)S(1)}, bf16[512,64]{0,1:T(8,128)(2,1)}, u32[]{:S(2)}) copy-start(bf16[512,64]{0,1:T(8,128)(2,1)} %param.21) | copy-start | bytes 196612
  11.9 0.9 copy-start.6
  106.0 4.5 %copy-start.10 = (bf16[32,512]{1,0:T(8,128)(2,1)S(1)}, bf16[32,512]{1,0:T(8,128)(2,1)}, u32[]{:S(2)}) copy-start(bf16[32,512]{1,0:T(8,128)(2,1)} %get-tuple-element.24) | copy-start | bytes 98308
  106.0 4.5 %copy-start = (bf16[1024,1024]{1,0:T(8,128)(2,1)S(1)}, bf16[1024,1024]{1,0:T(8,128)(2,1)}, u32[]{:S(2)}) copy-start(bf16[1024,1024]{1,0:T(8,128)(2,1)} %get-tuple-element.27.c_ref) | copy-start | bytes 6291460
  110.5 2.6 copy-start.2
  114.0 7.7 %copy-start.1 = (s32[1,1024]{1,0:T(1,128)S(1)}, s32[1,1024]{1,0:T(1,128)}, u32[]{:S(2)}) copy-start(s32[1,1024]{1,0:T(1,128)} %param.14) | copy-start | bytes 12292
  160.0 2.3 copy-start.12
  199.3 7.2 %copy-start.11 = (bf16[1024,2048]{1,0:T(8,128)(2,1)S(1)}, bf16[1024,2048]{1,0:T(8,128)(2,1)}, u32[]{:S(2)}) copy-start(bf16[1024,2048]{1,0:T(8,128)(2,1)} %get-tuple-element.29) | copy-start | bytes 12582916
  218.1 2.6 copy-start.5
  231.1 65.6 %copy-start.3 = (bf16[512,1024]{1,0:T(8,128)(2,1)S(1)}, bf16[512,1024]{1,0:T(8,128)(2,1)}, u32[]{:S(2)}) copy-start(bf16[512,1024]{1,0:T(8,128)(2,1)} %x_ref.1) | copy-start | bytes 3145732
  296.8 2.2 copy-start.4
